TPU v7x, 32 devices: a whole 2x2x4 slice. The times are simulated.
32 devices in a mesh: dp: 8 (over y, x, core), vocab: 4 (over z).
Axes of the slice: x: 2, y: 2, z: 4, core: 2. Of those that a mesh axis runs over, the one named last changes fastest.
Arguments:
- tokens: int32 [64, 512], P(('dp', 'vocab')), may hold values from 5 to 4100
- picks: int32 [64, 120], P(('dp', 'vocab')), may hold values from 0 to 512, as said below
- species: int32 [64], P(('dp', 'vocab')), may hold values from 0 to 7
- table: float32 [4104, 768], P('vocab', 'dp')
- table_m: float32 [4104, 768], P('vocab', 'dp'), may hold values from -1.9073486e-05 to 1.9073486e-05
- table_v: float32 [4104, 768], P('vocab', 'dp'), may hold values from 9.233324e-12 to 3.6933297e-11
- qkv_w: float32 [768, 2304], P(('dp', 'vocab')), may hold values from -0.21875 to 0.21875
- qkv_m: float32 [768, 2304], P(('dp', 'vocab')), may hold values from -1.9073486e-05 to 1.9073486e-05
- qkv_v: float32 [768, 2304], P(('dp', 'vocab')), may hold values from 9.233324e-12 to 3.6933297e-11
- out_w: float32 [768, 768], P(('dp', 'vocab')), may hold values from -1.75 to 1.75
- out_m: float32 [768, 768], P(('dp', 'vocab')), may hold values from -1.9073486e-05 to 1.9073486e-05
- out_v: float32 [768, 768], P(('dp', 'vocab')), may hold values from 9.233324e-12 to 3.6933297e-11
- up_w: float32 [768, 3072], P(('dp', 'vocab')), may hold values from -0.21875 to 0.21875
- up_m: float32 [768, 3072], P(('dp', 'vocab')), may hold values from -1.9073486e-05 to 1.9073486e-05
- up_v: float32 [768, 3072], P(('dp', 'vocab')), may hold values from 9.233324e-12 to 3.6933297e-11
- down_w: float32 [3072, 768], P(('dp', 'vocab')), may hold values from -0.109375 to 0.109375
- down_m: float32 [3072, 768], P(('dp', 'vocab')), may hold values from -1.9073486e-05 to 1.9073486e-05
- down_v: float32 [3072, 768], P(('dp', 'vocab')), may hold values from 9.233324e-12 to 3.6933297e-11
- trans_w: float32 [768, 768], P(('dp', 'vocab')), may hold values from -0.21875 to 0.21875
- trans_m: float32 [768, 768], P(('dp', 'vocab')), may hold values from -1.9073486e-05 to 1.9073486e-05
- trans_v: float32 [768, 768], P(('dp', 'vocab')), may hold values from 9.233324e-12 to 3.6933297e-11
- vectors: float32 [768, 14], P(('dp', 'vocab'))
- vectors_m: float32 [768, 14], P(('dp', 'vocab')), may hold values from -7.6293945e-05 to 7.6293945e-05
- vectors_v: float32 [768, 14], P(('dp', 'vocab')), may hold values from 1.4773319e-10 to 5.9093275e-10
Outputs:
- table_first: float32 [4104, 768], P('vocab', 'dp')
- table_second: float32 [4104, 768], P('vocab', 'dp')
- table_new: float32 [4104, 768], P('vocab', 'dp')
- table_copy: bfloat16 [4104, 768], P('vocab', 'dp')
- qkv_first: float32 [768, 2304], P(('dp', 'vocab'))
- qkv_second: float32 [768, 2304], P(('dp', 'vocab'))
- qkv_new: float32 [768, 2304], P(('dp', 'vocab'))
- qkv_copy: bfloat16 [768, 2304], P(('dp', 'vocab'))
- out_first: float32 [768, 768], P(('dp', 'vocab'))
- out_second: float32 [768, 768], P(('dp', 'vocab'))
- out_new: float32 [768, 768], P(('dp', 'vocab'))
- out_copy: bfloat16 [768, 768], P(('dp', 'vocab'))
- up_first: float32 [768, 3072], P(('dp', 'vocab'))
- up_second: float32 [768, 3072], P(('dp', 'vocab'))
- up_new: float32 [768, 3072], P(('dp', 'vocab'))
- up_copy: bfloat16 [768, 3072], P(('dp', 'vocab'))
- down_first: float32 [3072, 768], P(('dp', 'vocab'))
- down_second: float32 [3072, 768], P(('dp', 'vocab'))
- down_new: float32 [3072, 768], P(('dp', 'vocab'))
- down_copy: bfloat16 [3072, 768], P(('dp', 'vocab'))
- trans_first: float32 [768, 768], P(('dp', 'vocab'))
- trans_second: float32 [768, 768], P(('dp', 'vocab'))
- trans_new: float32 [768, 768], P(('dp', 'vocab'))
- trans_copy: bfloat16 [768, 768], P(('dp', 'vocab'))
- vectors_first: float32 [768, 14], P(('dp', 'vocab'))
- vectors_second: float32 [768, 14], P(('dp', 'vocab'))
- vectors_new: float32 [768, 14], P(('dp', 'vocab'))
- loss_sum: float32 [], replicated
- present: float32 [], replicated
- grad_norm: float32 [], replicated
Inputs may be any that keep to these rules, and one draw needn't show every extreme that they name: `picks`: each sequence's row lists whole masked spans of 6 consecutive positions (span starts are multiples of 6, spans disjoint), 6 entries a span, then 512 in every unused slot; some sequence fills all 120 slots.
All inputs are finite; a program needn't handle non-finite values.
Results may differ from a plain program's by a relative error of at most 0.018.
Values may be sent and summed in bfloat16 or wider, within the bound.
A program may use at most 192 MiB of HBM per device.

v0:
```python
import jax
import jax.numpy as jnp
from jax import lax
from jax.sharding import PartitionSpec as P

D = 768
HEADS = 12
HD = 64
NSPEC = 8
STEP = 10
VREAL = 4101


norm_eps = 1e-05
clip_limit = 0.01
matrix_rate = 0.06
vector_rate = 0.5
decay_rate = 0.01
adam_eps = 1e-08
floor_value = -1e30


def combined_all(value, axis, join):
    pieces = jax.tree.map(lambda part: lax.all_gather(part, axis), value)
    head = jax.tree.map(lambda part: part[0], pieces)
    tail = jax.tree.map(lambda part: part[1:], pieces)
    so_far, _ = lax.scan(lambda so_far, share: (join(so_far, share), None), head, tail)
    return so_far


def dot_low(left, right):
    return jnp.dot(left, right, preferred_element_type=jnp.float32)


def dot_left(left, right):
    return lax.dot_general(
        left, right, (((0,), (0,)), ((), ())), preferred_element_type=jnp.float32
    )


def dot_right(left, right):
    return lax.dot_general(
        left, right, (((1,), (1,)), ((), ())), preferred_element_type=jnp.float32
    )


def layernorm_forward(value, norm_gain, norm_shift):
    row_mean = jnp.mean(value, axis=-1, keepdims=True)
    centered_input = value - row_mean
    inverse_deviation = lax.rsqrt(
        jnp.mean(centered_input * centered_input, axis=-1, keepdims=True) + norm_eps
    )
    normalized_rows = centered_input * inverse_deviation
    return (normalized_rows * norm_gain + norm_shift, normalized_rows, inverse_deviation)


def layernorm_backward(gradient, normalized_rows, inverse_deviation, norm_gain):
    gain_gradient = jnp.sum(gradient * normalized_rows, axis=0)
    shift_gradient = jnp.sum(gradient, axis=0)
    normalized_gradient = gradient * norm_gain
    inner_argument = jnp.mean(
        normalized_gradient, axis=-1, keepdims=True
    ) + normalized_rows * jnp.mean(normalized_gradient * normalized_rows, axis=-1, keepdims=True)
    return (
        inverse_deviation * (normalized_gradient - inner_argument),
        gain_gradient,
        shift_gradient,
    )


def gelu_activation(value):
    return jax.nn.gelu(value, approximate=False)


def gelu_slope(value):
    cdf = 0.5 * (1.0 + lax.erf(value * 0.7071067811865476))
    return cdf + value * jnp.exp(-0.5 * value * value) * 0.3989422804014327


def split_heads(qkv_low):
    seq_len = qkv_low.shape[0]
    query = qkv_low[:, :D].reshape(seq_len, HEADS, HD)
    keys = qkv_low[:, D : 2 * D].reshape(seq_len, HEADS, HD)
    values = qkv_low[:, 2 * D :].reshape(seq_len, HEADS, HD)
    return (query, keys, values)


def attend_one(qkv_low):
    query, keys, values = split_heads(qkv_low)
    scores = jnp.einsum("qhd,khd->hqk", query, keys, preferred_element_type=jnp.float32) * HD ** (
        -0.5
    )
    top = jnp.max(scores, axis=-1, keepdims=True)
    expo = jnp.exp(scores - top)
    total = jnp.sum(expo, axis=-1, keepdims=True)
    probs = (expo / total).astype(jnp.bfloat16)
    result = jnp.einsum("hqk,khd->qhd", probs, values, preferred_element_type=jnp.float32)
    return (
        result.reshape(qkv_low.shape[0], D).astype(jnp.bfloat16),
        (top + jnp.log(total))[:, :, 0],
    )


def attend_back(items):
    qkv_low, grad_low, lse = items
    query, keys, values = split_heads(qkv_low)
    grad_heads = grad_low.reshape(qkv_low.shape[0], HEADS, HD)
    scores = jnp.einsum("qhd,khd->hqk", query, keys, preferred_element_type=jnp.float32) * HD ** (
        -0.5
    )
    probs = jnp.exp(scores - lse[:, :, None])
    d_probs = jnp.einsum("qhd,khd->hqk", grad_heads, values, preferred_element_type=jnp.float32)
    delta = jnp.sum(d_probs * probs, axis=-1, keepdims=True)
    d_scores = (probs * (d_probs - delta)).astype(jnp.bfloat16)
    d_query = jnp.einsum(
        "hqk,khd->qhd", d_scores, keys, preferred_element_type=jnp.float32
    ) * HD ** (-0.5)
    d_keys = jnp.einsum(
        "hqk,qhd->khd", d_scores, query, preferred_element_type=jnp.float32
    ) * HD ** (-0.5)
    d_values = jnp.einsum(
        "hqk,qhd->khd", probs.astype(jnp.bfloat16), grad_heads, preferred_element_type=jnp.float32
    )
    seq_len = qkv_low.shape[0]
    return jnp.concatenate(
        [d_query.reshape(seq_len, D), d_keys.reshape(seq_len, D), d_values.reshape(seq_len, D)],
        axis=1,
    )


def adamw(weight, first, second, gradient, rate):
    first = 0.5 * first + 0.5 * gradient
    second = 0.5 * second + 0.5 * gradient * gradient
    fix = 1.0 - 0.5**STEP
    step = first / fix / (jnp.sqrt(second / fix) + adam_eps)
    return (first, second, weight - rate * (step + decay_rate * weight))


def body(
    tokens,
    picks,
    species,
    table,
    table_m,
    table_v,
    qkv_w,
    qkv_m,
    qkv_v,
    out_w,
    out_m,
    out_v,
    up_w,
    up_m,
    up_v,
    down_w,
    down_m,
    down_v,
    trans_w,
    trans_m,
    trans_v,
    vectors,
    vectors_m,
    vectors_v,
):
    seqs, seq_len = tokens.shape
    vocab_rows = table.shape[0]
    vocab_start = lax.axis_index("vocab") * vocab_rows
    vocab_iota = jnp.arange(vocab_rows, dtype=jnp.int32)
    w_qkv, w_out, w_up, w_down, w_trans, vec_low = (
        lax.all_gather(qkv_w.astype(jnp.bfloat16), ("dp", "vocab"), axis=0, tiled=True),
        lax.all_gather(out_w.astype(jnp.bfloat16), ("dp", "vocab"), axis=0, tiled=True),
        lax.all_gather(up_w.astype(jnp.bfloat16), ("dp", "vocab"), axis=0, tiled=True),
        lax.all_gather(down_w.astype(jnp.bfloat16), ("dp", "vocab"), axis=0, tiled=True),
        lax.all_gather(trans_w.astype(jnp.bfloat16), ("dp", "vocab"), axis=0, tiled=True),
        lax.all_gather(vectors.astype(jnp.bfloat16), ("dp", "vocab"), axis=0, tiled=True),
    )
    vector_params = vec_low.astype(jnp.float32)
    table_low = lax.all_gather(table.astype(jnp.bfloat16), "dp", axis=1, tiled=True)
    positions = jnp.arange(seq_len, dtype=jnp.int32)
    masked = jnp.any(picks[:, :, None] == positions[None, None, :], axis=1)
    masked_flat = masked.reshape(-1)
    inputs = jnp.where(masked, -1, tokens).reshape(-1)
    live = (picks < seq_len).reshape(-1)
    spot = jnp.minimum(picks, seq_len - 1)
    row_index = (spot + jnp.arange(seqs, dtype=jnp.int32)[:, None] * seq_len).reshape(-1)
    row_target = jnp.take_along_axis(tokens, spot, axis=1).reshape(-1)
    row_species = jnp.broadcast_to(species[:, None], picks.shape).reshape(-1)
    row_live = live.astype(jnp.int32)
    ids_all, target_all, species_all, live_all = (
        lax.all_gather(inputs, "vocab", axis=0, tiled=True),
        lax.all_gather(row_target, "vocab", axis=0, tiled=True),
        lax.all_gather(row_species, "vocab", axis=0, tiled=True),
        lax.all_gather(row_live, "vocab", axis=0, tiled=True),
    )
    pick_rows = row_index.shape[0]
    rows = ids_all - vocab_start
    onehot = (rows[:, None] == vocab_iota[None, :]).astype(jnp.bfloat16)
    embedded_tokens = lax.psum_scatter(
        dot_low(onehot, table_low).astype(jnp.bfloat16), "vocab", scatter_dimension=0, tiled=True
    ).astype(jnp.float32)
    embedded_tokens = jnp.where(masked_flat[:, None], vector_params[:, 13], embedded_tokens)
    stream_zero, normalized_rows0, inverse_deviation0 = layernorm_forward(
        embedded_tokens, vector_params[:, 0], vector_params[:, 1]
    )
    x0_low = stream_zero.astype(jnp.bfloat16)
    qkv_bias = jnp.concatenate(
        [vector_params[:, 8], jnp.zeros((D,), jnp.float32), vector_params[:, 9]]
    )
    qkv_low = (dot_low(x0_low, w_qkv) + qkv_bias).astype(jnp.bfloat16)
    qkv_seqs = qkv_low.reshape(seqs, seq_len, 3 * D)
    attended, lse_attn = lax.map(attend_one, qkv_seqs)
    att_low = attended.reshape(-1, D)
    output_projection = dot_low(att_low, w_out) + vector_params[:, 10]
    stream_one, normalized_rows1, inverse_deviation1 = layernorm_forward(
        stream_zero + output_projection, vector_params[:, 2], vector_params[:, 3]
    )
    x1_low = stream_one.astype(jnp.bfloat16)
    hidden_pre = dot_low(x1_low, w_up)
    hidden_low = gelu_activation(hidden_pre).astype(jnp.bfloat16)
    feedforward_block = dot_low(hidden_low, w_down) + vector_params[:, 11]
    stream_two, normalized_rows2, inverse_deviation2 = layernorm_forward(
        stream_one + feedforward_block, vector_params[:, 4], vector_params[:, 5]
    )
    picked_low = stream_two[row_index].astype(jnp.bfloat16)
    transform_preactivation = dot_low(picked_low, w_trans) + vector_params[:, 12]
    latent_state, normalized_rows3, inverse_deviation3 = layernorm_forward(
        gelu_activation(transform_preactivation), vector_params[:, 6], vector_params[:, 7]
    )
    latent_all = lax.all_gather(latent_state.astype(jnp.bfloat16), "vocab", axis=0, tiled=True)
    column_ids = vocab_start + vocab_iota
    logits = dot_right(latent_all, table_low)
    logits = jnp.where(column_ids[None, :] < VREAL, logits, floor_value)
    local_top = jnp.max(logits, axis=-1)
    local_sum = jnp.sum(jnp.exp(logits - local_top[:, None]), axis=-1)
    is_target = column_ids[None, :] == target_all[:, None]
    local_hit = jnp.sum(jnp.where(is_target, logits, 0.0), axis=-1)

    def combine(first, second):
        top = jnp.maximum(first[0], second[0])
        total = first[1] * jnp.exp(first[0] - top) + second[1] * jnp.exp(second[0] - top)
        return (top, total, first[2] + second[2])

    top, total, hit_logit = combined_all((local_top, local_sum, local_hit), "vocab", combine)
    lse_rows = top + jnp.log(total)
    loss_rows = lse_rows - hit_logit
    own_loss = lax.dynamic_slice_in_dim(loss_rows, lax.axis_index("vocab") * pick_rows, pick_rows)
    species_iota = jnp.arange(NSPEC, dtype=jnp.int32)
    own_onehot = ((row_species[:, None] == species_iota[None, :]) & live[:, None]).astype(
        jnp.float32
    )
    species_loss = jnp.sum(own_onehot * own_loss[:, None], axis=0)
    species_count = jnp.sum(own_onehot, axis=0)
    loss_sums, counts = lax.psum((species_loss, species_count), ("dp", "vocab"))
    present_mask = counts > 0
    present = jnp.sum(present_mask.astype(jnp.float32))
    inverse = jnp.where(present_mask, 1.0 / jnp.maximum(counts, 1.0), 0.0) / present
    all_onehot = ((species_all[:, None] == species_iota[None, :]) & (live_all[:, None] > 0)).astype(
        jnp.float32
    )
    row_weight = jnp.sum(all_onehot * inverse[None, :], axis=-1)
    probs = jnp.exp(logits - lse_rows[:, None])
    d_logits = (row_weight[:, None] * (probs - is_target.astype(jnp.float32))).astype(jnp.bfloat16)
    table_grad = dot_left(d_logits, latent_all)
    latent_gradient = lax.psum_scatter(
        dot_low(d_logits, table_low).astype(jnp.bfloat16), "vocab", scatter_dimension=0, tiled=True
    ).astype(jnp.float32)
    gelu_input_gradient, grad_step_six, grad_step_seven = layernorm_backward(
        latent_gradient, normalized_rows3, inverse_deviation3, vector_params[:, 6]
    )
    d_trans_low = (gelu_input_gradient * gelu_slope(transform_preactivation)).astype(jnp.bfloat16)
    g_trans = dot_left(picked_low, d_trans_low)
    d12 = jnp.sum(d_trans_low.astype(jnp.float32), axis=0)
    d_picked = dot_right(d_trans_low, w_trans)
    stream_two_gradient = jnp.zeros_like(stream_two).at[row_index].add(d_picked)
    residual_two_gradient, grad_step_four, grad_step_five = layernorm_backward(
        stream_two_gradient, normalized_rows2, inverse_deviation2, vector_params[:, 4]
    )
    d_ffn_low = residual_two_gradient.astype(jnp.bfloat16)
    d11 = jnp.sum(d_ffn_low.astype(jnp.float32), axis=0)
    g_down = dot_left(hidden_low, d_ffn_low)
    d_hidden_low = (dot_right(d_ffn_low, w_down) * gelu_slope(hidden_pre)).astype(jnp.bfloat16)
    g_up = dot_left(x1_low, d_hidden_low)
    stream_one_gradient = residual_two_gradient + dot_right(d_hidden_low, w_up)
    residual_one_gradient, grad_step_two, grad_step_three = layernorm_backward(
        stream_one_gradient, normalized_rows1, inverse_deviation1, vector_params[:, 2]
    )
    d_proj_low = residual_one_gradient.astype(jnp.bfloat16)
    d10 = jnp.sum(d_proj_low.astype(jnp.float32), axis=0)
    g_out = dot_left(att_low, d_proj_low)
    d_att_low = dot_right(d_proj_low, w_out).astype(jnp.bfloat16)
    d_qkv = lax.map(attend_back, (qkv_seqs, d_att_low.reshape(seqs, seq_len, D), lse_attn))
    d_qkv_low = d_qkv.reshape(-1, 3 * D).astype(jnp.bfloat16)
    g_qkv = dot_left(x0_low, d_qkv_low)
    d_qkv_wide = d_qkv_low.astype(jnp.float32)
    d8 = jnp.sum(d_qkv_wide[:, :D], axis=0)
    d9 = jnp.sum(d_qkv_wide[:, 2 * D :], axis=0)
    stream_zero_gradient = residual_one_gradient + dot_right(d_qkv_low, w_qkv)
    embedded_gradient, grad_step_zero, grad_step_one = layernorm_backward(
        stream_zero_gradient, normalized_rows0, inverse_deviation0, vector_params[:, 0]
    )
    embedded_low = embedded_gradient.astype(jnp.bfloat16)
    mask_gradient = jnp.sum(
        jnp.where(masked_flat[:, None], embedded_low.astype(jnp.float32), 0.0), axis=0
    )
    rows = ids_all - vocab_start
    onehot = (rows[:, None] == vocab_iota[None, :]).astype(jnp.bfloat16)
    table_grad = table_grad + dot_left(
        onehot, lax.all_gather(embedded_low, "vocab", axis=0, tiled=True)
    )
    table_grad = lax.psum_scatter(
        table_grad.astype(jnp.bfloat16), "dp", scatter_dimension=1, tiled=True
    ).astype(jnp.float32)
    g_vec = jnp.stack(
        [
            grad_step_zero,
            grad_step_one,
            grad_step_two,
            grad_step_three,
            grad_step_four,
            grad_step_five,
            grad_step_six,
            grad_step_seven,
            d8,
            d9,
            d10,
            d11,
            d12,
            mask_gradient,
        ],
        axis=1,
    )
    shards = (
        lax.psum_scatter(g_qkv, ("dp", "vocab"), scatter_dimension=0, tiled=True),
        lax.psum_scatter(g_out, ("dp", "vocab"), scatter_dimension=0, tiled=True),
        lax.psum_scatter(g_up, ("dp", "vocab"), scatter_dimension=0, tiled=True),
        lax.psum_scatter(g_down, ("dp", "vocab"), scatter_dimension=0, tiled=True),
        lax.psum_scatter(g_trans, ("dp", "vocab"), scatter_dimension=0, tiled=True),
        lax.psum_scatter(g_vec, ("dp", "vocab"), scatter_dimension=0, tiled=True),
    )
    square = jnp.sum(table_grad * table_grad) + sum((jnp.sum(piece * piece) for piece in shards))
    grad_norm = jnp.sqrt(lax.psum(square, ("dp", "vocab")))
    factor = jnp.minimum(1.0, clip_limit / (grad_norm + 1e-06))
    masters = (table, qkv_w, out_w, up_w, down_w, trans_w, vectors)
    firsts = (table_m, qkv_m, out_m, up_m, down_m, trans_m, vectors_m)
    seconds = (table_v, qkv_v, out_v, up_v, down_v, trans_v, vectors_v)
    grads = (table_grad,) + tuple(shards)
    outs = []
    for index in range(7):
        rate = vector_rate if index == 6 else matrix_rate
        first, second, new = adamw(
            masters[index], firsts[index], seconds[index], grads[index] * factor, rate
        )
        outs.extend([first, second, new])
        if index < 6:
            outs.append(new.astype(jnp.bfloat16))
    loss_sum = jnp.sum(jnp.where(present_mask, loss_sums / jnp.maximum(counts, 1.0), 0.0))
    return (
        outs[0],
        outs[1],
        outs[2],
        outs[3],
        outs[4],
        outs[5],
        outs[6],
        outs[7],
        outs[8],
        outs[9],
        outs[10],
        outs[11],
        outs[12],
        outs[13],
        outs[14],
        outs[15],
        outs[16],
        outs[17],
        outs[18],
        outs[19],
        outs[20],
        outs[21],
        outs[22],
        outs[23],
        outs[24],
        outs[25],
        outs[26],
        loss_sum,
        present,
        grad_norm,
    )


def solution(mesh):
    in_specs = (
        P(("dp", "vocab"), None),
        P(("dp", "vocab"), None),
        P(("dp", "vocab")),
        P("vocab", "dp"),
        P("vocab", "dp"),
        P("vocab", "dp"),
        P(("dp", "vocab"), None),
        P(("dp", "vocab"), None),
        P(("dp", "vocab"), None),
        P(("dp", "vocab"), None),
        P(("dp", "vocab"), None),
        P(("dp", "vocab"), None),
        P(("dp", "vocab"), None),
        P(("dp", "vocab"), None),
        P(("dp", "vocab"), None),
        P(("dp", "vocab"), None),
        P(("dp", "vocab"), None),
        P(("dp", "vocab"), None),
        P(("dp", "vocab"), None),
        P(("dp", "vocab"), None),
        P(("dp", "vocab"), None),
        P(("dp", "vocab"), None),
        P(("dp", "vocab"), None),
        P(("dp", "vocab"), None),
    )
    out_specs = (
        P("vocab", "dp"),
        P("vocab", "dp"),
        P("vocab", "dp"),
        P("vocab", "dp"),
        P(("dp", "vocab"), None),
        P(("dp", "vocab"), None),
        P(("dp", "vocab"), None),
        P(("dp", "vocab"), None),
        P(("dp", "vocab"), None),
        P(("dp", "vocab"), None),
        P(("dp", "vocab"), None),
        P(("dp", "vocab"), None),
        P(("dp", "vocab"), None),
        P(("dp", "vocab"), None),
        P(("dp", "vocab"), None),
        P(("dp", "vocab"), None),
        P(("dp", "vocab"), None),
        P(("dp", "vocab"), None),
        P(("dp", "vocab"), None),
        P(("dp", "vocab"), None),
        P(("dp", "vocab"), None),
        P(("dp", "vocab"), None),
        P(("dp", "vocab"), None),
        P(("dp", "vocab"), None),
        P(("dp", "vocab"), None),
        P(("dp", "vocab"), None),
        P(("dp", "vocab"), None),
        P(),
        P(),
        P(),
    )
    return jax.shard_map(body, mesh=mesh, in_specs=in_specs, out_specs=out_specs, check_vma=False)
```

profile of v0, /device:TPU:0, one launch (start us, length us, event | category | flops | bytes accessed | tf_op | source)
XLA Modules:
  0.0 1485.1 jit_solution(10406426377219983853)
XLA Ops:
  11.4 14.8 all_gather.60
  26.2 14.4 all-gather.13.cloned.1.call-done
  62.6 73.8 %all-gather.3 = bf16[32,24,14]{1,2,0:T(8,128)(2,1)S(1)} all-gather(bf16[1,24,14]{1,2,0:T(8,128)(2,1)S(1)} %convert_bitcast_fusion), channel_id=1, replica_groups=mesh['dp'=8,'vocab'=4] {'dp','vocab'}, dimensions={0}, use_global_device_ids=true | all-gather | bytes 22176 | tf_op jit(solution)/shard_map/all_gather | solution.py:175
  137.6 30.6 %reduce-scatter.10.cloned.1.call-done = bf16[1024,768]{1,0:T(8,128)(2,1)} async-done(((bf16[4096,768]{1,0:T(8,128)(2,1)}), bf16[1024,768]{1,0:T(8,128)(2,1)}) %reduce-scatter.10.cloned.1.call-update) | async-done | bytes 1572880 | tf_op jit(solution)/shard_map/reduce_scatter | solution.py:198
  172.5 35.7 %all-gather.15.cloned.1.call-done = bf16[768,2304]{1,0:T(8,128)(2,1)} async-done(((bf16[24,2304]{1,0:T(8,128)(2,1)}), bf16[768,2304]{1,0:T(8,128)(2,1)}) %all-gather.15.cloned.1.call-update) | async-done | bytes 3538960 | tf_op jit(solution)/shard_map/all_gather | solution.py:170
  223.4 20.2 %while.36 = (s32[]{:T(128)}, bf16[2,512,768]{2,1,0:T(8,128)(2,1)}, f32[2,12,512]{2,1,0:T(8,128)S(1)}, bf16[2,512,2304]{1,2,0:T(8,128)(2,1)}, s32[]{:T(128)}) while((s32[]{:T(128)}, bf16[2,512,768]{2,1,0:T(8,128)(2,1)}, f32[2,12,512]{2,1,0:T(8,128)S(1)}, bf16[2,512,2304]{1,2,0:T(8,128)(2,1)}, s32[]{:T(128)}) %tuple.142), condition=%wide.region_11.12_spmd, body=%wide.region_8.11_spmd.sunk | while | flops 834004992 | bytes 53698640 | solution.py:211
  243.6 20.7 %all-gather.17.cloned.1.call-done = bf16[768,768]{1,0:T(8,128)(2,1)} async-done(((bf16[24,768]{1,0:T(8,128)(2,1)}), bf16[768,768]{1,0:T(8,128)(2,1)}) %all-gather.17.cloned.1.call-update) | async-done | bytes 1179664 | tf_op jit(solution)/shard_map/all_gather | solution.py:171
  269.0 61.2 %all-gather.19.cloned.1.call-done = bf16[768,3072]{1,0:T(8,128)(2,1)} async-done(((bf16[24,3072]{1,0:T(8,128)(2,1)}), bf16[768,3072]{1,0:T(8,128)(2,1)}) %all-gather.19.cloned.1.call-update) | async-done | bytes 4718608 | tf_op jit(solution)/shard_map/all_gather | solution.py:172
  330.3 37.2 %fusion.14 = (bf16[1024,3072]{1,0:T(8,128)(2,1)}, f32[1024,3072]{1,0:T(8,128)}) fusion(bf16[768,3072]{1,0:T(8,128)(2,1)} %all-gather.19.cloned.1.call-done, f32[1024,768]{1,0:T(8,128)S(1)} %get-tuple-element.304, f32[768]{0:T(1024)S(1)} %get-tuple-element.196, f32[768]{0:T(1024)S(1)} %get-tuple-element.197, f32[1024]{0:T(1024)S(1)} %add_rsqrt_fusion.1, ...), kind=kOutput, calls=%fused_computation.39 | convolution fusion | flops 5040242688 | bytes 26753024 | tf_op jit(solution)/shard_map/dot_general | solution.py:32
  367.4 28.3 %all-gather.21.cloned.1.call-done = bf16[3072,768]{1,0:T(8,128)(2,1)} async-done(((bf16[96,768]{1,0:T(8,128)(2,1)}), bf16[3072,768]{1,0:T(8,128)(2,1)}) %all-gather.21.cloned.1.call-update) | async-done | bytes 4718608 | tf_op jit(solution)/shard_map/all_gather | solution.py:173
  410.8 40.9 %all-gather.23.cloned.1.call-done = bf16[768,768]{1,0:T(8,128)(2,1)} async-done(((bf16[24,768]{1,0:T(8,128)(2,1)}), bf16[768,768]{1,0:T(8,128)(2,1)}) %all-gather.23.cloned.1.call-update) | async-done | bytes 1179664 | tf_op jit(solution)/shard_map/all_gather | solution.py:174
  461.4 18.2 %all-reduce.7 = (s32[960]{0:T(1024)S(1)}, s32[960]{0:T(1024)S(1)}, s32[960]{0:T(1024)S(1)}) all-reduce(s32[960]{0:T(1024)S(1)} %dynamic-update-slice.4, s32[960]{0:T(1024)S(1)} %dynamic-update-slice, s32[960]{0:T(1024)S(1)} %convert_dynamic-update-slice_fusion), channel_id=1, replica_groups=mesh['dp'=8,'vocab'=4] {'vocab'}, use_global_device_ids=true, to_apply=%add.4 | all-reduce | flops 2880 | bytes 23040
  501.7 17.4 %all-reduce.9 = (f32[3840]{0:T(1024)S(1)}, f32[3840]{0:T(1024)S(1)}, f32[3840]{0:T(1024)S(1)}) all-reduce(f32[3840]{0:T(1024)S(1)} %dynamic-update-slice.2, f32[3840]{0:T(1024)S(1)} %dynamic-update-slice.3, f32[3840]{0:T(1024)S(1)} %dynamic-update-slice.5), channel_id=2, replica_groups=mesh['dp'=8,'vocab'=4] {'vocab'}, use_global_device_ids=true, to_apply=%add.2 | all-reduce | flops 11520 | bytes 92160
  520.1 38.6 %all-reduce.8 = (f32[8]{0:T(128)S(1)}, f32[8]{0:T(128)S(1)}) all-reduce(f32[8]{0:T(128)S(1)} %get-tuple-element.205, f32[8]{0:T(128)S(1)} %get-tuple-element.204), channel_id=1, replica_groups=mesh['dp'=8,'vocab'=4] {'dp','vocab'}, use_global_device_ids=true, to_apply=%region_1.2 | all-reduce | flops 16 | bytes 128 | tf_op jit(solution)/shard_map/psum | solution.py:253
  567.2 33.7 %reduce-scatter.12.cloned.1.call-done = bf16[240,768]{1,0:T(8,128)(2,1)} async-done(((bf16[960,768]{1,0:T(8,128)(2,1)}), bf16[240,768]{1,0:T(8,128)(2,1)}) %reduce-scatter.12.cloned.1.call-update) | async-done | bytes 368656 | tf_op jit(solution)/shard_map/reduce_scatter | solution.py:264
  640.4 58.1 %while.38 = (s32[]{:T(128)}, bf16[2,512,2304]{2,1,0:T(8,128)(2,1)}, bf16[2,512,2304]{1,2,0:T(8,128)(2,1)}, f32[2,12,512]{2,1,0:T(8,128)S(1)}, bf16[2,512,768]{2,1,0:T(8,128)(2,1)S(1)}, /*index=5*/s32[]{:T(128)}) while((s32[]{:T(128)}, bf16[2,512,2304]{2,1,0:T(8,128)(2,1)}, bf16[2,512,2304]{1,2,0:T(8,128)(2,1)}, ...), condition=%wide.region_33.34_spmd, body=%wide.region_31.33_spmd.sunk | while | flops 2059659264 | bytes 141729952 | solution.py:291
  728.2 99.2 %all-gather.27.cloned.1.call-done = bf16[4096,768]{1,0:T(8,128)(2,1)} async-done(((bf16[1024,768]{1,0:T(8,128)(2,1)}), bf16[4096,768]{1,0:T(8,128)(2,1)}) %all-gather.27.cloned.1.call-update) | async-done | bytes 6291472 | tf_op jit(solution)/shard_map/all_gather | solution.py:308
  873.5 39.0 %all-reduce.6 = f32[768,14]{0,1:T(8,128)S(1)} all-reduce(f32[768,14]{0,1:T(8,128)S(1)} %stack.59), channel_id=13, replica_groups=mesh['dp'=8,'vocab'=4] {'dp','vocab'}, use_global_device_ids=true, to_apply=%region_62.63.clone | all-reduce | flops 10752 | bytes 86016
  914.8 58.3 %reduce-scatter.18.cloned.1.call-done = f32[24,768]{1,0:T(8,128)} async-done(((f32[768,768]{1,0:T(8,128)}), f32[24,768]{1,0:T(8,128)}) %reduce-scatter.18.cloned.1.call-update) | async-done | bytes 73744 | tf_op jit(solution)/shard_map/reduce_scatter | solution.py:334
  974.6 122.8 %reduce-scatter.16.cloned.1.call-done = f32[24,2304]{1,0:T(8,128)} async-done(((f32[768,2304]{1,0:T(8,128)}), f32[24,2304]{1,0:T(8,128)}) %reduce-scatter.16.cloned.1.call-update) | async-done | bytes 221200 | tf_op jit(solution)/shard_map/reduce_scatter | solution.py:333
  1100.3 38.7 %reduce-scatter.14.cloned.1.call-done = bf16[1026,96]{0,1:T(8,128)(2,1)} async-done(((bf16[1026,768]{0,1:T(8,128)(2,1)}), bf16[1026,96]{0,1:T(8,128)(2,1)}) %reduce-scatter.14.cloned.1.call-update) | async-done | bytes 197008 | tf_op jit(solution)/shard_map/reduce_scatter | solution.py:310
  1140.7 140.0 %reduce-scatter.20.cloned.1.call-done = f32[24,3072]{1,0:T(8,128)} async-done(((f32[768,3072]{1,0:T(8,128)}), f32[24,3072]{1,0:T(8,128)}) %reduce-scatter.20.cloned.1.call-update) | async-done | bytes 294928 | tf_op jit(solution)/shard_map/reduce_scatter | solution.py:335
  1283.0 138.9 %reduce-scatter.22.cloned.1.call-done = f32[96,768]{1,0:T(8,128)} async-done(((f32[3072,768]{1,0:T(8,128)}), f32[96,768]{1,0:T(8,128)}) %reduce-scatter.22.cloned.1.call-update) | async-done | bytes 294928 | tf_op jit(solution)/shard_map/reduce_scatter | solution.py:336
  1426.3 39.7 %psum.22 = f32[]{:T(128)} all-reduce(f32[]{:T(128)S(6)} %add.449), channel_id=1, replica_groups=mesh['dp'=8,'vocab'=4] {'dp','vocab'}, use_global_device_ids=true, to_apply=%region_64.65 | all-reduce | flops 1 | bytes 8 | tf_op jit(solution)/shard_map/psum | solution.py:341
  (450 shorter events, 317.7 us)
Async XLA Ops:
  8.0 32.5 %all-gather.13.cloned.1.call-start = ((), (), s32[]{:S(2)}) async-start(), calls=%async_computation.8 | async-start | bytes 1990656 | tf_op jit(solution)/shard_map/all_gather | solution.py:178
  9.8 158.3 %reduce-scatter.10.cloned.1.call-start = ((), (), s32[]{:S(2)}) async-start(), calls=%async_computation.9 | async-start | bytes 7864320 | tf_op jit(solution)/shard_map/reduce_scatter | solution.py:198
  52.6 155.6 %all-gather.15.cloned.1.call-start = ((), (), s32[]{:S(2)}) async-start(), calls=%async_computation.10 | async-start | bytes 3649536 | tf_op jit(solution)/shard_map/all_gather | solution.py:170
  54.1 210.2 %all-gather.17.cloned.1.call-start = ((), (), s32[]{:S(2)}) async-start(), calls=%async_computation.11 | async-start | bytes 1216512 | tf_op jit(solution)/shard_map/all_gather | solution.py:171
  54.8 275.5 %all-gather.19.cloned.1.call-start = ((), (), s32[]{:S(2)}) async-start(), calls=%async_computation.12 | async-start | bytes 4866048 | tf_op jit(solution)/shard_map/all_gather | solution.py:172
  55.6 340.2 %all-gather.21.cloned.1.call-start = ((), (), s32[]{:S(2)}) async-start(), calls=%async_computation.13 | async-start | bytes 4866048 | tf_op jit(solution)/shard_map/all_gather | solution.py:173
  56.3 395.3 %all-gather.23.cloned.1.call-start = ((), (), s32[]{:S(2)}) async-start(), calls=%async_computation.14 | async-start | bytes 1216512 | tf_op jit(solution)/shard_map/all_gather | solution.py:174
  57.1 435.1 %all-gather.25.cloned.1.call-start = ((), (), s32[]{:S(2)}) async-start(), calls=%async_computation.15 | async-start | bytes 1843200 | tf_op jit(solution)/shard_map/all_gather | solution.py:229
  457.3 143.6 %reduce-scatter.12.cloned.1.call-start = ((), (), s32[]{:S(2)}) async-start(), calls=%async_computation.16 | async-start | bytes 1843200 | tf_op jit(solution)/shard_map/reduce_scatter | solution.py:264
  567.1 260.4 %all-gather.27.cloned.1.call-start = ((), (), s32[]{:S(2)}) async-start(), calls=%async_computation.17 | async-start | bytes 7864320 | tf_op jit(solution)/shard_map/all_gather | solution.py:308
  710.9 202.4 %reduce-scatter.24.cloned.1.call-start = ((), (), s32[]{:S(2)}) async-start(), calls=%async_computation.23 | async-start | bytes 2433024 | tf_op jit(solution)/shard_map/reduce_scatter | solution.py:337
  712.9 260.2 %reduce-scatter.18.cloned.1.call-start = ((), (), s32[]{:S(2)}) async-start(), calls=%async_computation.20 | async-start | bytes 2433024 | tf_op jit(solution)/shard_map/reduce_scatter | solution.py:334
  718.2 379.2 %reduce-scatter.16.cloned.1.call-start = ((), (), s32[]{:S(2)}) async-start(), calls=%async_computation.19 | async-start | bytes 7299072 | tf_op jit(solution)/shard_map/reduce_scatter | solution.py:333
  728.2 410.9 %reduce-scatter.14.cloned.1.call-start = ((), (), s32[]{:S(2)}) async-start(), calls=%async_computation.18 | async-start | bytes 1990656 | tf_op jit(solution)/shard_map/reduce_scatter | solution.py:310
  845.7 435.0 %reduce-scatter.20.cloned.1.call-start = ((), (), s32[]{:S(2)}) async-start(), calls=%async_computation.21 | async-start | bytes 9732096 | tf_op jit(solution)/shard_map/reduce_scatter | solution.py:335
  856.4 565.5 %reduce-scatter.22.cloned.1.call-start = ((), (), s32[]{:S(2)}) async-start(), calls=%async_computation.22 | async-start | bytes 9732096 | tf_op jit(solution)/shard_map/reduce_scatter | solution.py:336
  873.0 596.1 %copy-start.42 = (f32[24,768]{1,0:T(8,128)S(1)}, f32[24,768]{1,0:T(8,128)}, u32[]{:S(2)}) copy-start(f32[24,768]{1,0:T(8,128)} %param.39) | copy-start | bytes 221188
  873.0 596.1 %copy-start.51 = (f32[24,768]{1,0:T(8,128)S(1)}, f32[24,768]{1,0:T(8,128)}, u32[]{:S(2)}) copy-start(f32[24,768]{1,0:T(8,128)} %param.41) | copy-start | bytes 221188
  873.0 597.7 %copy-start.28 = (f32[24,2304]{1,0:T(8,128)S(1)}, f32[24,2304]{1,0:T(8,128)}, u32[]{:S(2)}) copy-start(f32[24,2304]{1,0:T(8,128)} %param.36) | copy-start | bytes 663556
  873.0 597.7 %copy-start.45 = (f32[24,2304]{1,0:T(8,128)S(1)}, f32[24,2304]{1,0:T(8,128)}, u32[]{:S(2)}) copy-start(f32[24,2304]{1,0:T(8,128)} %param.38) | copy-start | bytes 663556
  873.0 597.7 %copy-start.46 = (f32[24,2304]{1,0:T(8,128)S(1)}, f32[24,2304]{1,0:T(8,128)}, u32[]{:S(2)}) copy-start(f32[24,2304]{1,0:T(8,128)} %param.37) | copy-start | bytes 663556
  873.4 599.4 %copy-start.20 = (f32[24,3072]{1,0:T(8,128)S(1)}, f32[24,3072]{1,0:T(8,128)}, u32[]{:S(2)}) copy-start(f32[24,3072]{1,0:T(8,128)} %param.42) | copy-start | bytes 884740
  873.4 599.4 %copy-start.35 = (f32[24,3072]{1,0:T(8,128)S(1)}, f32[24,3072]{1,0:T(8,128)}, u32[]{:S(2)}) copy-start(f32[24,3072]{1,0:T(8,128)} %param.44) | copy-start | bytes 884740
  873.4 599.4 %copy-start.36 = (f32[24,3072]{1,0:T(8,128)S(1)}, f32[24,3072]{1,0:T(8,128)}, u32[]{:S(2)}) copy-start(f32[24,3072]{1,0:T(8,128)} %param.43) | copy-start | bytes 884740
  (97 other events, 9971.6 us)
Sparse Core Ops, SparseCore 0:
  11.3 29.2 all-gather.12
  52.7 115.4 reduce-scatter.9
  457.4 34.7 all-gather.24
  567.2 33.6 reduce-scatter.11
  711.0 116.4 all-gather.26
Sparse Core Ops, SparseCore 1:
  56.4 151.7 all-gather.14
  211.4 52.8 all-gather.16
  267.5 62.7 all-gather.18
  333.7 62.0 all-gather.20
  399.2 52.4 all-gather.22
  717.8 152.0 reduce-scatter.23
  875.0 98.0 reduce-scatter.17
  979.6 117.7 reduce-scatter.15
  1100.6 38.3 reduce-scatter.13
  1145.0 135.7 reduce-scatter.19
  1287.5 134.5 reduce-scatter.21
where the time goes:
time: 1490 us
  waiting for transfers between devices  876 us (59%)
  blocking collectives  242 us (16%)
  matrix products  211 us (14%)
  other arithmetic  81.7 us (5%)
  local copies, waits for them, and re-layouts  48.1 us (3%)
  between operations  24.9 us (2%)
    reduce_scatter x1, waiting for transfers between devices, body(): lax.psum_scatter(g_up, ('dp', 'vocab'), scatter_dimension=0, tiled=True)  140 us
    reduce_scatter x1, waiting for transfers between devices, body(): lax.psum_scatter(g_down, ('dp', 'vocab'), scatter_dimension=0, tiled=True)  139 us
    reduce_scatter x1, waiting for transfers between devices, body(): lax.psum_scatter(g_qkv, ('dp', 'vocab'), scatter_dimension=0, tiled=True)  123 us
    all_gather x1, waiting for transfers between devices, body(): lax.all_gather(embedded_low, 'vocab', axis=0, tiled=True)  99.2 us
    dot_general x7, matrix products, dot_low(): return jnp.dot(left, right, preferred_element_type=jnp.float32)  81.8 us
    unnamed x3, blocking collectives  74.7 us
    all_gather x1, blocking collectives, body(): lax.all_gather(vectors.astype(jnp.bfloat16), ('dp', 'vocab'), axis=0, til...  73.8 us
    all_gather x1, waiting for transfers between devices, body(): lax.all_gather(up_w.astype(jnp.bfloat16), ('dp', 'vocab'), axis=0, tiled=...  61.2 us
  transfers between devices with their start and end apart: 16, of which 15 were waited for; matrix products, arithmetic and copies ran while one was open for 12% of the time, Pallas kernels for 0%

commit v1 on v0

v1 whole, which is shorter than its diff:
```python
import functools

import jax
import jax.numpy as jnp
from jax import lax
from jax.experimental import pallas as pl
from jax.experimental.pallas import tpu as pltpu
from jax.sharding import PartitionSpec as P

D = 768
HEADS = 12
HD = 64
FF = 3072
NSPEC = 8
NVEC = 14
STEP = 10
VREAL = 4101
MESH = pl.DeviceIdType.MESH
BF = jnp.bfloat16
F32 = jnp.float32

norm_eps = 1e-05
clip_limit = 0.01
matrix_rate = 0.06
vector_rate = 0.5
decay_rate = 0.01
adam_eps = 1e-08
floor_value = -1e30

VEC_AT = 3 * D
OUT_AT = VEC_AT + 256
UP_AT = OUT_AT + D
TRANS_AT = UP_AT + FF
JOIN = TRANS_AT + D
JOIN_PARTS = (
    (0, 1280, True),
    (1280, 1280, False),
    (OUT_AT, 768, True),
    (UP_AT, 1536, False),
    (UP_AT + 1536, 1536, True),
    (TRANS_AT, 768, False),
)
VMEM_LIMIT = 62 * 2**20


def padded(rows):
    return -(-rows // 128) * 128


def pack_parts(value):
    pieces = []
    for first, width, _ in JOIN_PARTS:
        half = width // 2
        pieces.append(
            jnp.concatenate([value[:, first : first + half], value[:, first + half : first + width]], axis=0)
        )
    return jnp.concatenate(pieces, axis=1)


def unpack_parts(value):
    rows = value.shape[0] // 2
    pieces = []
    for first, width, _ in JOIN_PARTS:
        at = first // 2
        piece = value[:, at : at + width // 2]
        pieces += [piece[:rows], piece[rows:]]
    return jnp.concatenate(pieces, axis=1)


class Place:
    def __init__(self, n_vocab):
        dp = lax.axis_index("dp")
        z = lax.axis_index("vocab")
        core = lax.rem(dp, 2)
        bit_x = lax.rem(lax.div(dp, 2), 2)
        bit_y = lax.div(dp, 4)
        self.dp, self.z, self.core, self.n_vocab = dp, z, core, n_vocab
        self.step_core = 1 - 2 * core
        self.step_x = 2 - 4 * bit_x
        self.step_y = 4 - 8 * bit_y

    def across(self, which):
        return self.dp + {"core": self.step_core, "x": self.step_x, "y": self.step_y}[which]

    def device(self, which):
        return (self.across(which), self.z)

    def along(self, k):
        return lax.rem(self.z + k, self.n_vocab)

    def greet(self):
        barrier = pltpu.get_barrier_semaphore()
        for which in ("core", "x", "y"):
            pl.semaphore_signal(barrier, inc=1, device_id=self.device(which), device_id_type=MESH)
        for k in range(1, self.n_vocab):
            pl.semaphore_signal(barrier, inc=1, device_id=(self.dp, self.along(k)), device_id_type=MESH)
        pl.semaphore_wait(barrier, 3 + self.n_vocab - 1)


def remote(src, dst, send, recv, device):
    return pltpu.make_async_remote_copy(
        src_ref=src, dst_ref=dst, send_sem=send, recv_sem=recv, device_id=device, device_id_type=MESH
    )


def block_view(ref, stride, offset, rows, first, width):
    def view(index):
        return ref.at[pl.ds(pl.multiple_of(index * stride + offset, 16), rows), pl.ds(first, width)]

    return view


def tile_sum(place, tile_ref, land, ring, send, recv):
    for i, which in enumerate(("core", "x", "y")):
        copy = remote(tile_ref, land.at[i], send.at[i], recv.at[i], place.device(which))
        copy.start()
        copy.wait()
        tile_ref[...] = tile_ref[...] + land[i]
    ring[place.z] = tile_ref[...]
    copies = []
    for k in range(1, place.n_vocab):
        copy = remote(
            tile_ref, ring.at[place.z], send.at[2 + k], recv.at[2 + k], (place.dp, place.along(k))
        )
        copy.start()
        copies.append(copy)
    for copy in copies:
        copy.wait()
    total = ring[0]
    for k in range(1, place.n_vocab):
        total = total + ring[k]
    return total


def gather_kernel(
    n_vocab, packed_ref, table_ref, down_ref, tile_in,
    join_out, down_out, table_out, tile_out,
    join, down, table, stage, tile, land, ring,
    z_send, z_recv, d_send, d_recv, out_sem, t_send, t_recv,
):
    place = Place(n_vocab)
    place.greet()
    dp, z = place.dp, place.z
    t_rows, t_cols = table_ref.shape
    rows = packed_ref.shape[0] // 2
    d_rows = down_ref.shape[0]
    started = []

    def go(copy):
        copy.start()
        started.append(copy)

    chunks = []
    z_slot = 0

    def along_z(slot, src, dst):
        for k in range(1, n_vocab):
            go(remote(src, dst, z_send.at[slot, k - 1], z_recv.at[slot, k - 1], (dp, place.along(k))))

    def wait_z(slot, src, dst):
        for k in range(1, n_vocab):
            remote(src, dst, z_send.at[slot, k - 1], z_recv.at[slot, k - 1], (dp, place.along(k))).wait_recv()

    def nothing():
        pass

    sub = t_rows // 3
    for j in range(3):
        src = table_ref.at[pl.ds(sub * j, sub), :]
        dst = table.at[
            pl.ds(pl.multiple_of(dp * t_rows + sub * j, 16), sub), pl.ds(pl.multiple_of(z * t_cols, 128), t_cols)
        ]
        along_z(z_slot, src, dst)
        half = n_vocab * t_cols // 2
        ready = functools.partial(wait_z, z_slot, src, dst)
        chunks.append((block_view(table, t_rows, sub * j, sub, 0, half), True, ready))
        chunks.append((block_view(table, t_rows, sub * j, sub, half, half), False, nothing))
        z_slot += 1
    table[
        pl.ds(pl.multiple_of(dp * t_rows, 16), t_rows), pl.ds(pl.multiple_of(z * t_cols, 128), t_cols)
    ] = table_ref[...]

    def assemble(first, width):
        half = width // 2
        at = first // 2
        lefts, rights = [], []
        for k in range(n_vocab):
            piece = stage[k, :, at : at + half].astype(F32)
            lefts.append(piece[:rows])
            rights.append(piece[rows:])
        where = pl.ds(pl.multiple_of(dp * rows * n_vocab, 16), rows * n_vocab)
        join[where, first : first + half] = jnp.concatenate(lefts, axis=0).astype(BF)
        join[where, first + half : first + width] = jnp.concatenate(rights, axis=0).astype(BF)

    def join_ready(slot, src, dst, first, width):
        wait_z(slot, src, dst)
        assemble(first, width)

    stage[z] = packed_ref[...]
    for first, width, x_first in JOIN_PARTS:
        src = packed_ref.at[:, pl.ds(first // 2, width // 2)]
        dst = stage.at[z, :, pl.ds(first // 2, width // 2)]
        along_z(z_slot, src, dst)
        ready = functools.partial(join_ready, z_slot, src, dst, first, width)
        chunks.append((block_view(join, rows * n_vocab, 0, rows * n_vocab, first, width), x_first, ready))
        z_slot += 1
    down[pl.ds(pl.multiple_of((dp * n_vocab + z) * d_rows, 16), d_rows), :] = down_ref[...]
    for j in range(2):
        half = D // 2
        src = down_ref.at[:, pl.ds(half * j, half)]
        dst = down.at[pl.ds(pl.multiple_of((dp * n_vocab + z) * d_rows, 16), d_rows), pl.ds(half * j, half)]
        along_z(z_slot, src, dst)
        ready = functools.partial(wait_z, z_slot, src, dst)
        chunks.append((block_view(down, d_rows * n_vocab, 0, d_rows * n_vocab, half * j, half), j == 0, ready))
        z_slot += 1

    tile[...] = tile_in[...]
    tile_out[...] = tile_sum(place, tile, land, ring, t_send, t_recv)

    def moves(i):
        view, x_first, _ = chunks[i]
        one, two = ("x", "y") if x_first else ("y", "x")
        own = dp
        a = place.across(one)
        b = place.across(two)
        ab = a + b - own

        def move(k, block, which):
            return remote(view(block), view(block), d_send.at[i, k], d_recv.at[i, k], place.device(which))

        flip = place.step_core
        sends = (
            move(0, own, one), move(1, own, two), move(2, a, two), move(3, own, "core"),
            move(4, a, "core"), move(5, b, "core"), move(6, ab, "core"),
        )
        arrivals = (
            move(0, a, one), move(1, b, two), move(2, ab, two), move(3, own + flip, "core"),
            move(4, a + flip, "core"), move(5, b + flip, "core"), move(6, ab + flip, "core"),
        )
        return sends, arrivals

    every = [moves(i) for i in range(len(chunks))]
    n = len(chunks)
    for turn in range(n + 3):
        i = turn
        if i < n:
            chunks[i][2]()
            sends, _ = every[i]
            go(sends[0])
            go(sends[1])
            go(sends[3])
        i = turn - 1
        if 0 <= i < n:
            sends, arrivals = every[i]
            arrivals[0].wait_recv()
            go(sends[2])
            go(sends[4])
        i = turn - 2
        if 0 <= i < n:
            sends, arrivals = every[i]
            arrivals[1].wait_recv()
            go(sends[5])
            arrivals[2].wait_recv()
            go(sends[6])
        i = turn - 3
        if 0 <= i < n:
            _, arrivals = every[i]
            for k in range(3, 7):
                arrivals[k].wait_recv()
    outs = [
        pltpu.make_async_copy(join, join_out, out_sem.at[0]),
        pltpu.make_async_copy(down, down_out, out_sem.at[1]),
        pltpu.make_async_copy(table, table_out, out_sem.at[2]),
    ]
    for copy in outs:
        copy.start()
    for copy in started:
        copy.wait_send()
    for copy in outs:
        copy.wait()


def gather_all(packed, table_t, down, tile, n_dp, n_vocab):
    rows = packed.shape[0] // 2 * n_vocab * n_dp
    t_rows, t_cols = table_t.shape
    join_shape = (rows, JOIN)
    down_shape = (down.shape[0] * n_vocab * n_dp, D)
    table_shape = (t_rows * n_dp, t_cols * n_vocab)
    n_chunks = 6 + len(JOIN_PARTS) + 2
    slots = 3 + len(JOIN_PARTS) + 2
    vmem = pl.BlockSpec(memory_space=pltpu.VMEM)
    anywhere = pl.BlockSpec(memory_space=pl.ANY)
    return pl.pallas_call(
        functools.partial(gather_kernel, n_vocab),
        out_shape=(
            jax.ShapeDtypeStruct(join_shape, BF),
            jax.ShapeDtypeStruct(down_shape, BF),
            jax.ShapeDtypeStruct(table_shape, BF),
            jax.ShapeDtypeStruct(tile.shape, F32),
        ),
        in_specs=[vmem] * 4,
        out_specs=(anywhere, anywhere, anywhere, vmem),
        scratch_shapes=[
            pltpu.VMEM(join_shape, BF),
            pltpu.VMEM(down_shape, BF),
            pltpu.VMEM(table_shape, BF),
            pltpu.VMEM((n_vocab,) + packed.shape, BF),
            pltpu.VMEM(tile.shape, F32),
            pltpu.VMEM((3,) + tile.shape, F32),
            pltpu.VMEM((n_vocab,) + tile.shape, F32),
            pltpu.SemaphoreType.DMA((slots, n_vocab - 1)),
            pltpu.SemaphoreType.DMA((slots, n_vocab - 1)),
            pltpu.SemaphoreType.DMA((n_chunks, 7)),
            pltpu.SemaphoreType.DMA((n_chunks, 7)),
            pltpu.SemaphoreType.DMA((3,)),
            pltpu.SemaphoreType.DMA((2 + n_vocab,)),
            pltpu.SemaphoreType.DMA((2 + n_vocab,)),
        ],
        compiler_params=pltpu.CompilerParams(
            collective_id=0, has_side_effects=True, vmem_limit_bytes=VMEM_LIMIT
        ),
    )(packed, table_t, down, tile)


def reduce_kernel(
    n_vocab, join_in, down_in, table_in, tile_in,
    join_out, down_out, table_out, tile_out,
    join, down, table, *rest,
):
    n_join = len(JOIN_PARTS)
    n_chunks = 6 + n_join + 2
    from_core = rest[:n_chunks]
    from_two = rest[n_chunks : 2 * n_chunks]
    from_one = rest[2 * n_chunks : 3 * n_chunks]
    (packed, z_join, z_down, z_table, tile, land, ring,
     in_sem, z_send, z_recv, d_send, d_recv, t_send, t_recv) = rest[3 * n_chunks :]
    place = Place(n_vocab)
    loads = [
        pltpu.make_async_copy(join_in, join, in_sem.at[0]),
        pltpu.make_async_copy(down_in, down, in_sem.at[1]),
        pltpu.make_async_copy(table_in, table, in_sem.at[2]),
    ]
    for copy in loads:
        copy.start()
    place.greet()
    dp, z = place.dp, place.z
    t_rows, t_cols = table_out.shape
    rows = join_out.shape[0] // 2
    d_rows = down_out.shape[0]
    sub = t_rows // 3
    started = []

    def go(copy):
        copy.start()
        started.append(copy)

    chunks = []
    for first, width, x_first in JOIN_PARTS:
        chunks.append((block_view(join, rows * n_vocab, 0, rows * n_vocab, first, width), x_first, 0))
    for j in range(2):
        half = D // 2
        chunks.append((block_view(down, d_rows * n_vocab, 0, d_rows * n_vocab, half * j, half), j == 0, 1))
    for j in range(3):
        half = n_vocab * t_cols // 2
        chunks.append((block_view(table, t_rows, sub * j, sub, 0, half), True, 2))
        chunks.append((block_view(table, t_rows, sub * j, sub, half, half), False, 2))

    def add_into(target, source):
        size = target.shape[0]

        def step(i, carry):
            at = pl.ds(pl.multiple_of(i * 16, 16), 16)
            target[at, :] = target[at, :] + source[at, :]
            return carry

        lax.fori_loop(0, size // 16, step, 0)

    def names(i):
        one, two = ("x", "y") if chunks[i][1] else ("y", "x")
        own = dp
        a = place.across(one)
        b = place.across(two)
        return one, two, (own, a, b, a + b - own)

    def to_core(i):
        view = chunks[i][0]
        _, _, blocks = names(i)
        return [
            remote(
                view(block + place.step_core), from_core[i].at[k], d_send.at[i, k], d_recv.at[i, k],
                place.device("core"),
            )
            for k, block in enumerate(blocks)
        ]

    def to_two(i):
        view = chunks[i][0]
        _, two, (own, a, b, ab) = names(i)
        return [
            remote(view(block), from_two[i].at[k], d_send.at[i, 4 + k], d_recv.at[i, 4 + k], place.device(two))
            for k, block in enumerate((b, ab))
        ]

    def to_one(i):
        view = chunks[i][0]
        one, _, (own, a, b, ab) = names(i)
        return [remote(view(a), from_one[i], d_send.at[i, 6], d_recv.at[i, 6], place.device(one))]

    def z_copies(slot, src_of, dst_of):
        return [
            remote(
                src_of(place.along(k)), dst_of(k - 1), z_send.at[slot, k - 1], z_recv.at[slot, k - 1],
                (dp, place.along(k)),
            )
            for k in range(1, n_vocab)
        ]

    def join_pack(first, width):
        half = width // 2
        at = first // 2
        block = join[
            pl.ds(pl.multiple_of(dp * rows * n_vocab, 16), rows * n_vocab), first : first + width
        ].astype(F32)
        for k in range(n_vocab):
            piece = block[k * rows : (k + 1) * rows]
            packed[k, :, at : at + half] = jnp.concatenate([piece[:, :half], piece[:, half:]], axis=0).astype(BF)

    z_jobs = []

    def finish(i):
        if i < n_join:
            first, width, _ = JOIN_PARTS[i]
            join_pack(first, width)
            cols = pl.ds(first // 2, width // 2)
            copies = z_copies(i, lambda to: packed.at[to, :, cols], lambda k: z_join.at[k, :, cols])
        elif i < n_join + 2:
            cols = pl.ds((i - n_join) * (D // 2), D // 2)
            copies = z_copies(
                i,
                lambda to: down.at[pl.ds(pl.multiple_of((dp * n_vocab + to) * d_rows, 16), d_rows), cols],
                lambda k: z_down.at[k, :, cols],
            )
        else:
            j = i - n_join - 2
            if j % 2 == 0:
                return
            j = j // 2
            copies = z_copies(
                n_join + 2 + j,
                lambda to: table.at[
                    pl.ds(pl.multiple_of(dp * t_rows + sub * j, 16), sub),
                    pl.ds(pl.multiple_of(to * t_cols, 128), t_cols),
                ],
                lambda k: z_table.at[k, pl.ds(sub * j, sub), :],
            )
        for copy in copies:
            go(copy)
        z_jobs.append(copies)

    n = n_chunks
    for turn in range(n + 3):
        i = turn
        if i < n:
            if i == 0:
                loads[0].wait()
            if i == n_join:
                loads[1].wait()
            if i == n_join + 2:
                loads[2].wait()
            for copy in to_core(i):
                go(copy)
        i = turn - 1
        if 0 <= i < n:
            view = chunks[i][0]
            _, _, (own, a, b, ab) = names(i)
            arrivals = to_core(i)
            for k, block in ((2, b), (3, ab)):
                arrivals[k].wait_recv()
                add_into(view(block), from_core[i].at[k])
            for copy in to_two(i):
                go(copy)
            for k, block in ((0, own), (1, a)):
                arrivals[k].wait_recv()
                add_into(view(block), from_core[i].at[k])
        i = turn - 2
        if 0 <= i < n:
            view = chunks[i][0]
            _, _, (own, a, b, ab) = names(i)
            arrivals = to_two(i)
            arrivals[1].wait_recv()
            add_into(view(a), from_two[i].at[1])
            for copy in to_one(i):
                go(copy)
            arrivals[0].wait_recv()
            add_into(view(own), from_two[i].at[0])
        i = turn - 3
        if 0 <= i < n:
            view = chunks[i][0]
            to_one(i)[0].wait_recv()
            add_into(view(dp), from_one[i])
            finish(i)
    for copies in z_jobs:
        for copy in copies:
            copy.wait_recv()
    square = jnp.zeros((), F32)
    whole = packed[z].astype(F32)
    for k in range(n_vocab - 1):
        whole = whole + z_join[k].astype(F32)
    join_out[...] = whole
    square = square + jnp.sum(whole * whole)
    whole = down[pl.ds(pl.multiple_of((dp * n_vocab + z) * d_rows, 16), d_rows), :].astype(F32)
    for k in range(n_vocab - 1):
        whole = whole + z_down[k].astype(F32)
    down_out[...] = whole
    square = square + jnp.sum(whole * whole)
    whole = table[
        pl.ds(pl.multiple_of(dp * t_rows, 16), t_rows), pl.ds(pl.multiple_of(z * t_cols, 128), t_cols)
    ].astype(F32)
    for k in range(n_vocab - 1):
        whole = whole + z_table[k].astype(F32)
    table_out[...] = whole
    square = square + jnp.sum(whole * whole)
    row = lax.broadcasted_iota(jnp.int32, tile.shape, 0)
    tile[...] = jnp.where(row == 0, square, tile_in[...])
    tile_out[...] = tile_sum(place, tile, land, ring, t_send, t_recv)
    for copy in started:
        copy.wait_send()


def reduce_all(g_join, g_down, g_table, tile, n_dp, n_vocab):
    rows = g_join.shape[0] // (n_dp * n_vocab)
    d_rows = g_down.shape[0] // (n_dp * n_vocab)
    t_rows = g_table.shape[0] // n_dp
    t_cols = g_table.shape[1] // n_vocab
    shapes = [(rows * n_vocab, width) for _, width, _ in JOIN_PARTS]
    shapes += [(d_rows * n_vocab, D // 2)] * 2
    shapes += [(t_rows // 3, n_vocab * t_cols // 2)] * 6
    slots = len(JOIN_PARTS) + 5
    vmem = pl.BlockSpec(memory_space=pltpu.VMEM)
    anywhere = pl.BlockSpec(memory_space=pl.ANY)
    dma = pltpu.SemaphoreType.DMA
    return pl.pallas_call(
        functools.partial(reduce_kernel, n_vocab),
        out_shape=(
            jax.ShapeDtypeStruct((2 * rows, JOIN // 2), F32),
            jax.ShapeDtypeStruct((d_rows, D), F32),
            jax.ShapeDtypeStruct((t_rows, t_cols), F32),
            jax.ShapeDtypeStruct(tile.shape, F32),
        ),
        in_specs=[anywhere, anywhere, anywhere, vmem],
        out_specs=(vmem,) * 4,
        scratch_shapes=[
            pltpu.VMEM(g_join.shape, BF),
            pltpu.VMEM(g_down.shape, BF),
            pltpu.VMEM(g_table.shape, BF),
        ]
        + [pltpu.VMEM((4,) + shape, BF) for shape in shapes]
        + [pltpu.VMEM((2,) + shape, BF) for shape in shapes]
        + [pltpu.VMEM(shape, BF) for shape in shapes]
        + [
            pltpu.VMEM((n_vocab, 2 * rows, JOIN // 2), BF),
            pltpu.VMEM((n_vocab - 1, 2 * rows, JOIN // 2), BF),
            pltpu.VMEM((n_vocab - 1, d_rows, D), BF),
            pltpu.VMEM((n_vocab - 1, t_rows, t_cols), BF),
            pltpu.VMEM(tile.shape, F32),
            pltpu.VMEM((3,) + tile.shape, F32),
            pltpu.VMEM((n_vocab,) + tile.shape, F32),
            dma((3,)),
            dma((slots, n_vocab - 1)),
            dma((slots, n_vocab - 1)),
            dma((len(shapes), 7)),
            dma((len(shapes), 7)),
            dma((2 + n_vocab,)),
            dma((2 + n_vocab,)),
        ],
        compiler_params=pltpu.CompilerParams(
            collective_id=1, has_side_effects=True, vmem_limit_bytes=VMEM_LIMIT
        ),
    )(g_join, g_down, g_table, tile)


def dot_low(left, right):
    return jnp.dot(left, right, preferred_element_type=F32)


def dot_left(left, right):
    return lax.dot_general(left, right, (((0,), (0,)), ((), ())), preferred_element_type=F32)


def dot_right(left, right):
    return lax.dot_general(left, right, (((1,), (1,)), ((), ())), preferred_element_type=F32)


def norm_forward(value, gain, shift):
    mean = jnp.mean(value, axis=-1, keepdims=True)
    centered = value - mean
    inverse = lax.rsqrt(jnp.mean(centered * centered, axis=-1, keepdims=True) + norm_eps)
    normal = centered * inverse
    return normal * gain + shift, normal, inverse


def norm_backward(gradient, normal, inverse, gain):
    gain_gradient = jnp.sum(gradient * normal, axis=0)
    shift_gradient = jnp.sum(gradient, axis=0)
    scaled = gradient * gain
    inner = jnp.mean(scaled, axis=-1, keepdims=True) + normal * jnp.mean(
        scaled * normal, axis=-1, keepdims=True
    )
    return inverse * (scaled - inner), gain_gradient, shift_gradient


def gelu(value):
    return 0.5 * value * (1.0 + lax.erf(value * 0.7071067811865476))


def gelu_slope(value):
    cdf = 0.5 * (1.0 + lax.erf(value * 0.7071067811865476))
    return cdf + value * jnp.exp(-0.5 * value * value) * 0.3989422804014327


def species_counts(picks, species, seq_len):
    live = (picks < seq_len).astype(F32)
    kinds = jnp.arange(NSPEC, dtype=jnp.int32)
    return jnp.sum((species[:, None] == kinds[None, :]).astype(F32) * jnp.sum(live, axis=1)[:, None], axis=0)


def local_step(tokens, picks, species, counts, join, down, table_t, block, wide):
    seqs, seq_len = tokens.shape
    slots = picks.shape[1]
    w_qkv = join[:, : 3 * D]
    vec = join[:, VEC_AT : VEC_AT + NVEC].astype(F32)
    w_out = join[:, OUT_AT : OUT_AT + D]
    w_up = join[:, UP_AT : UP_AT + FF]
    w_trans = join[:, TRANS_AT : TRANS_AT + D]

    masked = jnp.any(picks[:, :, None] == jnp.arange(seq_len, dtype=jnp.int32)[None, None, :], axis=1)
    masked_flat = masked.reshape(-1)
    live = (picks < seq_len).reshape(-1)
    spot = jnp.minimum(picks, seq_len - 1)
    row_index = (spot + jnp.arange(seqs, dtype=jnp.int32)[:, None] * seq_len).reshape(-1)
    target = jnp.take_along_axis(tokens, spot, axis=1).reshape(-1)
    row_species = jnp.broadcast_to(species[:, None], picks.shape).reshape(-1)

    cols = jnp.arange(table_t.shape[1], dtype=jnp.int32)
    col_real = cols % wide < block
    col_id = jnp.where(col_real, cols // wide * block + cols % wide, -1)
    inputs = jnp.where(masked, -2, tokens).reshape(-1)
    onehot = (inputs[:, None] == col_id[None, :]).astype(BF)
    embedded = jnp.where(masked_flat[:, None], vec[:, 13], dot_right(onehot, table_t))
    stream_zero, normal0, inverse0 = norm_forward(embedded, vec[:, 0], vec[:, 1])
    x0_low = stream_zero.astype(BF)
    keys = dot_low(x0_low, w_qkv[:, D : 2 * D]).astype(BF)
    values = (dot_low(x0_low, w_qkv[:, 2 * D :]) + vec[:, 9]).astype(BF)
    x0_rows = stream_zero[row_index]
    x0_rows_low = x0_rows.astype(BF)
    query = (dot_low(x0_rows_low, w_qkv[:, :D]) + vec[:, 8]).astype(BF)
    q4 = query.reshape(seqs, slots, HEADS, HD)
    k4 = keys.reshape(seqs, seq_len, HEADS, HD)
    v4 = values.reshape(seqs, seq_len, HEADS, HD)
    scores = jnp.einsum("sqhd,skhd->shqk", q4, k4, preferred_element_type=F32) * HD ** (-0.5)
    probs = jax.nn.softmax(scores, axis=-1)
    probs_low = probs.astype(BF)
    att = jnp.einsum("shqk,skhd->sqhd", probs_low, v4, preferred_element_type=F32)
    att_low = att.reshape(-1, D).astype(BF)
    stream_one, normal1, inverse1 = norm_forward(
        x0_rows + dot_low(att_low, w_out) + vec[:, 10], vec[:, 2], vec[:, 3]
    )
    x1_low = stream_one.astype(BF)
    hidden = dot_low(x1_low, w_up)
    hidden_low = gelu(hidden).astype(BF)
    stream_two, normal2, inverse2 = norm_forward(
        stream_one + dot_low(hidden_low, down) + vec[:, 11], vec[:, 4], vec[:, 5]
    )
    picked_low = stream_two.astype(BF)
    trans = dot_low(picked_low, w_trans) + vec[:, 12]
    latent, normal3, inverse3 = norm_forward(gelu(trans), vec[:, 6], vec[:, 7])
    latent_low = latent.astype(BF)
    logits = dot_low(latent_low, table_t)
    logits = jnp.where((col_real & (col_id < VREAL))[None, :], logits, floor_value)
    top = jnp.max(logits, axis=-1, keepdims=True)
    expo = jnp.exp(logits - top)
    total = jnp.sum(expo, axis=-1, keepdims=True)
    is_target = col_id[None, :] == target[:, None]
    hit = jnp.sum(jnp.where(is_target, logits, 0.0), axis=-1)
    loss_rows = (top + jnp.log(total))[:, 0] - hit
    kinds = jnp.arange(NSPEC, dtype=jnp.int32)
    own = ((row_species[:, None] == kinds[None, :]) & live[:, None]).astype(F32)
    species_loss = jnp.sum(own * loss_rows[:, None], axis=0)
    present_mask = counts > 0
    present = jnp.sum(present_mask.astype(F32))
    inverse = jnp.where(present_mask, 1.0 / jnp.maximum(counts, 1.0), 0.0) / present
    weight = jnp.sum(own * inverse[None, :], axis=-1)
    loss_part = jnp.sum(jnp.where(present_mask, species_loss / jnp.maximum(counts, 1.0), 0.0))
    d_logits = (weight[:, None] * (expo / total - is_target.astype(F32))).astype(BF)

    d_latent = dot_right(d_logits, table_t)
    d_act, d6, d7 = norm_backward(d_latent, normal3, inverse3, vec[:, 6])
    d_trans = (d_act * gelu_slope(trans)).astype(BF)
    g_trans = dot_left(picked_low, d_trans)
    d12 = jnp.sum(d_trans.astype(F32), axis=0)
    d_two, d4, d5 = norm_backward(dot_right(d_trans, w_trans), normal2, inverse2, vec[:, 4])
    d_ffn = d_two.astype(BF)
    d11 = jnp.sum(d_ffn.astype(F32), axis=0)
    g_down = dot_left(hidden_low, d_ffn)
    d_hidden = (dot_right(d_ffn, down) * gelu_slope(hidden)).astype(BF)
    g_up = dot_left(x1_low, d_hidden)
    d_one, d2, d3 = norm_backward(d_two + dot_right(d_hidden, w_up), normal1, inverse1, vec[:, 2])
    d_proj = d_one.astype(BF)
    d10 = jnp.sum(d_proj.astype(F32), axis=0)
    g_out = dot_left(att_low, d_proj)
    d_att = dot_right(d_proj, w_out).astype(BF).reshape(seqs, slots, HEADS, HD)
    d_probs = jnp.einsum("sqhd,skhd->shqk", d_att, v4, preferred_element_type=F32)
    delta = jnp.sum(d_probs * probs, axis=-1, keepdims=True)
    d_scores = (probs * (d_probs - delta)).astype(BF)
    d_q = jnp.einsum("shqk,skhd->sqhd", d_scores, k4, preferred_element_type=F32) * HD ** (-0.5)
    d_k = jnp.einsum("shqk,sqhd->skhd", d_scores, q4, preferred_element_type=F32) * HD ** (-0.5)
    d_v = jnp.einsum("shqk,sqhd->skhd", probs_low, d_att, preferred_element_type=F32)
    d_q = d_q.reshape(-1, D).astype(BF)
    d_k = d_k.reshape(-1, D).astype(BF)
    d_v = d_v.reshape(-1, D).astype(BF)
    d8 = jnp.sum(d_q.astype(F32), axis=0)
    d9 = jnp.sum(d_v.astype(F32), axis=0)
    g_q = dot_left(x0_rows_low, d_q)
    g_k = dot_left(x0_low, d_k)
    g_v = dot_left(x0_low, d_v)
    d_rows = d_one + dot_right(d_q, w_qkv[:, :D])
    d_zero = dot_right(d_k, w_qkv[:, D : 2 * D]) + dot_right(d_v, w_qkv[:, 2 * D :])
    d_zero = d_zero.at[row_index].add(jnp.where(live[:, None], d_rows, 0.0))
    d_emb, d0, d1 = norm_backward(d_zero, normal0, inverse0, vec[:, 0])
    d_emb_low = d_emb.astype(BF)
    d13 = jnp.sum(jnp.where(masked_flat[:, None], d_emb_low.astype(F32), 0.0), axis=0)
    g_table = dot_left(latent_low, d_logits) + dot_left(d_emb_low, onehot)
    g_vec = jnp.stack([d0, d1, d2, d3, d4, d5, d6, d7, d8, d9, d10, d11, d12, d13], axis=1)
    g_vec = jnp.pad(g_vec, ((0, 0), (0, OUT_AT - VEC_AT - NVEC)))
    g_join = jnp.concatenate([g_q, g_k, g_v, g_vec, g_out, g_up, g_trans], axis=1)
    return loss_part, present, g_join.astype(BF), g_down.astype(BF), g_table.astype(BF)


def adamw(weight, first, second, gradient, rate):
    first = 0.5 * first + 0.5 * gradient
    second = 0.5 * second + 0.5 * gradient * gradient
    fix = 1.0 - 0.5**STEP
    step = first / fix / (jnp.sqrt(second / fix) + adam_eps)
    return (first, second, weight - rate * (step + decay_rate * weight))


def body(
    n_dp, n_vocab, tokens, picks, species,
    table, table_m, table_v, qkv_w, qkv_m, qkv_v, out_w, out_m, out_v, up_w, up_m, up_v,
    down_w, down_m, down_v, trans_w, trans_m, trans_v, vectors, vectors_m, vectors_v,
):
    block, columns = table.shape
    wide = padded(block)
    rows = qkv_w.shape[0]
    own_kernels = n_dp == 8 and rows % 8 == 0 and columns % 48 == 0
    joined = jnp.concatenate(
        [qkv_w, jnp.pad(vectors, ((0, 0), (0, OUT_AT - VEC_AT - NVEC))), out_w, up_w, trans_w], axis=1
    ).astype(BF)
    down_low = down_w.astype(BF)
    table_t = jnp.pad(table.T.astype(BF), ((0, 0), (0, wide - block)))
    counts = species_counts(picks, species, tokens.shape[1])
    if own_kernels:
        tile = jnp.broadcast_to(jnp.pad(counts, (0, 128 - NSPEC))[None, :], (8, 128))
        join_all, down_all, table_all, tile = gather_all(
            pack_parts(joined), table_t, down_low, tile, n_dp, n_vocab
        )
        counts = tile[0, :NSPEC]
    else:
        both = ("dp", "vocab")
        join_all = lax.all_gather(joined, both, axis=0, tiled=True)
        down_all = lax.all_gather(down_low, both, axis=0, tiled=True)
        table_all = lax.all_gather(table_t, "vocab", axis=1, tiled=True)
        table_all = lax.all_gather(table_all, "dp", axis=0, tiled=True)
        counts = lax.psum(counts, both)
    loss, present, g_join, g_down, g_table = local_step(
        tokens, picks, species, counts, join_all, down_all, table_all, block, wide
    )
    if own_kernels:
        tile = jnp.full((8, 128), loss, F32)
        g_join, g_down, g_table, tile = reduce_all(g_join, g_down, g_table, tile, n_dp, n_vocab)
        g_join = unpack_parts(g_join)
        square, loss_sum = tile[0, 0], tile[1, 0]
    else:
        g_join = lax.psum_scatter(g_join.astype(F32), both, scatter_dimension=0, tiled=True)
        g_down = lax.psum_scatter(g_down.astype(F32), both, scatter_dimension=0, tiled=True)
        g_table = lax.psum_scatter(g_table, "dp", scatter_dimension=0, tiled=True)
        g_table = lax.psum_scatter(g_table, "vocab", scatter_dimension=1, tiled=True).astype(F32)
        square = jnp.sum(g_join * g_join) + jnp.sum(g_down * g_down) + jnp.sum(g_table * g_table)
        square, loss_sum = lax.psum((square, loss), both)
    grad_norm = jnp.sqrt(square)
    factor = jnp.minimum(1.0, clip_limit / (grad_norm + 1e-06))
    grads = (
        g_table[:, :block].T, g_join[:, : 3 * D], g_join[:, OUT_AT : OUT_AT + D], g_join[:, UP_AT : UP_AT + FF],
        g_down, g_join[:, TRANS_AT:], g_join[:, VEC_AT : VEC_AT + NVEC],
    )
    masters = (table, qkv_w, out_w, up_w, down_w, trans_w, vectors)
    firsts = (table_m, qkv_m, out_m, up_m, down_m, trans_m, vectors_m)
    seconds = (table_v, qkv_v, out_v, up_v, down_v, trans_v, vectors_v)
    outs = []
    for index in range(7):
        rate = vector_rate if index == 6 else matrix_rate
        first, second, new = adamw(masters[index], firsts[index], seconds[index], grads[index] * factor, rate)
        outs.extend([first, second, new])
        if index < 6:
            outs.append(new.astype(BF))
    return tuple(outs) + (loss_sum, present, grad_norm)


def solution(mesh):
    both = P(("dp", "vocab"), None)
    split = P("vocab", "dp")
    in_specs = (both, both, P(("dp", "vocab"))) + (split,) * 3 + (both,) * 18
    out_specs = (split,) * 4 + (both,) * 23 + (P(),) * 3
    step = functools.partial(body, mesh.shape["dp"], mesh.shape["vocab"])
    return jax.shard_map(step, mesh=mesh, in_specs=in_specs, out_specs=out_specs, check_vma=False)
```

time: 1490 us -> 573 us (0.38)
  waiting for transfers between devices: 876 us -> 0 us
  Pallas kernels: 0 us -> 305 us
  blocking collectives: 242 us -> 0 us
  matrix products: 211 us -> 140 us
  other arithmetic: 81.7 us -> 48.4 us
  local copies, waits for them, and re-layouts: 48.1 us -> 69.4 us
  between operations: 24.9 us -> 4.52 us
    reduce_scatter x8 -> x0, waiting for transfers between devices: 563 us -> none  [the longest x1 140 us: body(): lax.psum_scatter(g_up, ('dp', 'vocab'), scatter_dimension=0, tiled=True)]
    all_gather x8 -> x0, waiting for transfers between devices: 313 us -> none  [the longest x1 99.2 us: body(): lax.all_gather(embedded_low, 'vocab', axis=0, tiled=True)]
    pallas_call x0 -> x2, Pallas kernels: none -> 305 us  [the longest x1 174 us: gather_all(): pl.pallas_call(functools.partial(gather_kernel, n_vocab), out_shape=(jax....]
    all_gather x2 -> x0, blocking collectives: 88.6 us -> none  [the longest x1 73.8 us: body(): lax.all_gather(vectors.astype(jnp.bfloat16), ('dp', 'vocab'), axis=0, til...]
    psum x2 -> x0, blocking collectives: 78.3 us -> none  [the longest x1 39.7 us: body(): grad_norm = jnp.sqrt(lax.psum(square, ('dp', 'vocab')))]
    unnamed x3 -> x0, blocking collectives: 74.7 us -> none
    dot_general x21 -> x14, matrix products: 118 us -> 59.8 us  [the longest x8 27.2 us: dot_low(): return jnp.dot(left, right, preferred_element_type=F32)]
    reduce_sum x25 -> x16, other arithmetic: 39.1 us -> 16.6 us  [the longest x1 3.52 us: local_step(): hit = jnp.sum(jnp.where(is_target, logits, 0.0), axis=-1)]
  transfers between devices with their start and end apart: 16 -> 0, of which waited for: 15 -> 0; matrix products, arithmetic and copies ran while one was open for 12% -> 0% of each run, Pallas kernels for 0% -> 0%
where the time goes in v1:
time: 573 us; the launch traced here: 567 us
  Pallas kernels  305 us (53%)
  matrix products  140 us (24%)
  local copies, waits for them, and re-layouts  69.4 us (12%)
  other arithmetic  48.4 us (8%)
    pallas_call x1, Pallas kernels, gather_all(): pl.pallas_call(functools.partial(gather_kernel, n_vocab), out_shape=(jax....  174 us
    pallas_call x1, Pallas kernels, reduce_all(): pl.pallas_call(functools.partial(reduce_kernel, n_vocab), out_shape=(jax....  131 us
    dot_general x9, matrix products, dot_right(): lax.dot_general(left, right, (((1,), (1,)), ((), ())), preferred_element_...  40.6 us
    dot_general x9, matrix products, dot_left(): lax.dot_general(left, right, (((0,), (0,)), ((), ())), preferred_element_...  39.7 us
    dot_general x8, matrix products, dot_low(): return jnp.dot(left, right, preferred_element_type=F32)  27.2 us
    dot_general x1, matrix products, local_step(): jnp.einsum('shqk,sqhd->skhd', probs_low, d_att, preferred_element_type=F32)  11.7 us
    unnamed x262, local copies, waits for them, and re-layouts  11.5 us

profile of v1, /device:TPU:0, one launch (start us, length us, event | category | flops | bytes accessed | tf_op | source)
XLA Modules:
  0.0 567.1 jit_solution(16626169508896387949)
XLA Ops:
  10.5 173.9 %shard_map.463 = (bf16[768,7168]{1,0:T(8,128)(2,1)}, bf16[3072,768]{1,0:T(8,128)(2,1)}, bf16[768,4608]{1,0:T(8,128)(2,1)}, f32[8,128]{1,0:T(8,128)}) custom-call(bf16[48,3584]{1,0:T(8,128)(2,1)} %copy-done.37, bf16[96,1152]{1,0:T(8,128)(2,1)} %pad.19.table_ref, bf16[96,768]{1,0:T(8,128)(2,1)} %convert_element_type.176.down_ref, ...), custom_call_target="tpu_custom_call" | custom-call | tf_op jit(solution)/shard_map/pallas_call | solution.py:293
  189.0 10.2 %select_reduce_fusion.1 = (f32[1024]{0:T(1024)S(1)}, f32[1024,768]{0,1:T(8,128)S(1)}) fusion(f32[768]{0:T(1024)S(1)} %get-tuple-element.226, pred[1024]{0:T(1024)(128)(4,1)S(1)} %broadcast_in_dim.63, bf16[768,4608]{1,0:T(8,128)(2,1)} %get-tuple-element.39, s32[4608]{0:T(1024)S(1)} %fusion.110, s32[1024]{0:T(1024)S(1)} %bitcast.100), kind=kOutput, calls=%fused_computation.55 | convolution fusion | flops 7254047744 | bytes 10254336 | tf_op jit(solution)/shard_map/dot_general | solution.py:591
  203.2 3.9 add_convert_fusion.1
  209.7 3.9 reshape.293
  221.4 4.1 gather_fusion
  229.6 4.5 convolution_convert_fusion.3
  236.7 4.3 reshape.291
  243.4 4.7 fusion.161
  248.1 10.1 %fusion.62 = bf16[2,120,12,64]{1,3,2,0:T(8,128)(2,1)S(1)} fusion(bf16[2,512,12,64]{1,0,3,2:T(2,128)(2,1)} %reshape.293, f32[2,12,120]{2,1,0:T(8,128)} %get-tuple-element.300, f32[2,12,120,512]{3,2,1,0:T(8,128)} %copy-done.1), kind=kOutput, calls=%fused_computation.94 | convolution fusion | flops 196304192 | bytes 7851264 | tf_op jit(solution)/shard_map/shqk,skhd->sqhd/dot_general | solution.py:663
  263.2 5.6 multiply_convert_fusion.3
  274.9 4.3 fusion.164
  286.0 8.0 %multiply_reduce_fusion.6 = (bf16[768]{0:T(1024)(128)(2,1)}, f32[240]{0:T(256)S(1)}, f32[240]{0:T(256)S(1)}, bf16[768]{0:T(1024)(128)(2,1)}, f32[240,768]{1,0:T(8,128)S(1)}) fusion(f32[240,768]{1,0:T(8,128)} %copy-done.22, f32[240]{0:T(256)S(1)} %add_rsqrt_fusion.1, f32[240]{0:T(256)S(1)} %broadcast_multiply_fusion.9, f32[768]{0:T(1024)S(1)} %copy-done.68, ...), kind=kOutput, calls=%fused_computation.114 | convolution fusion | flops 1708091392 | bytes 13008384 | tf_op jit(solution)/shard_map/dot_general | solution.py:591
  298.8 4.3 fusion.22
  310.5 5.1 multiply_reduce_fusion
  330.7 4.5 fusion.76
  335.2 11.7 %fusion.166 = (bf16[12,64]{1,0:T(8,128)(2,1)}, bf16[2,12,64,512]{3,2,1,0:T(8,128)(2,1)}) fusion(f32[2,12,120]{2,1,0:T(8,128)} %get-tuple-element.300, f32[2,12,120,512]{3,2,1,0:T(8,128)} %copy-done.1, bf16[2,120,12,64]{1,0,3,2:T(2,128)(2,1)} %reshape.295), kind=kOutput, calls=%fused_computation.295 | convolution fusion | flops 197691968 | bytes 7852800 | tf_op jit(solution)/shard_map/shqk,sqhd->skhd/dot_general | solution.py:717
  352.0 4.5 convolution_add_fusion
  356.4 6.3 %scatter_fusion = f32[1024,768]{1,0:T(8,128)} fusion(f32[1024,768]{1,0:T(8,128)} %convolution_add_fusion, s32[240]{0:T(256)} %bitcast.99, f32[240,768]{1,0:T(8,128)} %fusion.47), kind=kCustom, calls=%fused_computation.2 | custom fusion | flops 184320 | bytes 2212800 | tf_op jit(solution)/shard_map/scatter-add | solution.py:728
  371.2 10.4 %fusion.1 = f32[768,4608]{1,0:T(8,128)} fusion(bf16[1024,768]{0,1:T(8,128)(2,1)S(1)} %get-tuple-element.257, s32[4608]{0:T(1024)S(1)} %copy-done.53, s32[1024]{0:T(1024)S(1)} %bitcast.101), kind=kOutput, calls=%fused_computation.4 | convolution fusion | flops 7252475904 | bytes 15751168 | tf_op jit(solution)/shard_map/dot_general | solution.py:587
  381.7 8.8 %add_convert_fusion.table_in = bf16[768,4608]{1,0:T(8,128)(2,1)} fusion(f32[768,4608]{1,0:T(8,128)} %fusion.1, f32[240,768]{1,0:T(8,128)S(1)} %copy-done.24, f32[768]{0:T(1024)S(1)} %copy-done.104, f32[768]{0:T(1024)S(1)} %copy-done.69, f32[240]{0:T(256)S(1)} %copy-done.89, f32[240]{0:T(256)S(1)} %copy-done.76, f32[240,4608]{1,0:T(8,128)S(1)} %bitcast.89, ...), kind=kOutput, calls=%fused_computation.8 | convolution fusion | flops 1714434048 | bytes 26424960 | tf_op jit(solution)/shard_map/dot_general | solution.py:587
  401.4 4.6 fusion.31
  411.1 3.8 fusion.10
  416.7 3.6 convolution_convert_fusion.down_in
  421.6 130.8 %shard_map.464 = (f32[48,3584]{1,0:T(8,128)}, f32[96,768]{1,0:T(8,128)}, f32[96,1152]{1,0:T(8,128)}, f32[8,128]{1,0:T(8,128)}) custom-call(bf16[768,7168]{1,0:T(8,128)(2,1)} %fusion.28.join_in, bf16[3072,768]{1,0:T(8,128)(2,1)} %convolution_convert_fusion.down_in, bf16[768,4608]{1,0:T(8,128)(2,1)} %add_convert_fusion.table_in, f32[8,128]{1,0:T(8,128)} %broadcast_in_dim.80.tile_in), custom_call_target="tpu_custom_call" | custom-call | tf_op jit(solution)/shard_map/pallas_call | solution.py:542
  (400 shorter events, 126.9 us)
Async XLA Ops:
  188.9 10.8 %copy-start.60 = (pred[1024]{0:T(1024)(128)(4,1)}, pred[1024]{0:T(1024)(128)(4,1)S(1)}, u32[]{:S(2)}) copy-start(pred[1024]{0:T(1024)(128)(4,1)S(1)} %broadcast_in_dim.63) | copy-start | bytes 3076
  229.6 11.4 %copy-start.16 = (bf16[2,120,12,64]{1,0,3,2:T(2,128)(2,1)}, bf16[2,120,12,64]{1,0,3,2:T(2,128)(2,1)S(1)}, u32[]{:S(2)}) copy-start(bf16[2,120,12,64]{1,0,3,2:T(2,128)(2,1)S(1)} %reshape.292) | copy-start | bytes 1105924
  270.4 27.5 %copy-start.73 = (f32[240]{0:T(256)}, f32[240]{0:T(256)S(1)}, u32[]{:S(2)}) copy-start(f32[240]{0:T(256)S(1)} %broadcast_multiply_fusion.10) | copy-start | bytes 2884
  270.7 27.2 %copy-start.86 = (f32[240]{0:T(256)}, f32[240]{0:T(256)S(1)}, u32[]{:S(2)}) copy-start(f32[240]{0:T(256)S(1)} %add_rsqrt_fusion.2) | copy-start | bytes 2884
  274.5 19.5 %copy-start.75 = (f32[240]{0:T(256)}, f32[240]{0:T(256)S(1)}, u32[]{:S(2)}) copy-start(f32[240]{0:T(256)S(1)} %broadcast_multiply_fusion.9) | copy-start | bytes 2884
  274.7 19.3 %copy-start.88 = (f32[240]{0:T(256)}, f32[240]{0:T(256)S(1)}, u32[]{:S(2)}) copy-start(f32[240]{0:T(256)S(1)} %add_rsqrt_fusion.1) | copy-start | bytes 2884
  279.2 14.8 %copy-start.92 = (f32[240]{0:T(256)}, f32[240]{0:T(256)S(1)}, u32[]{:S(2)}) copy-start(f32[240]{0:T(256)S(1)} %get-tuple-element.309) | copy-start | bytes 2884
  279.3 14.7 %copy-start.90 = (s32[240]{0:T(256)}, s32[240]{0:T(256)S(1)}, u32[]{:S(2)}) copy-start(s32[240]{0:T(256)S(1)} %select_n.119) | copy-start | bytes 2884
  282.8 11.2 %copy-start.94 = (f32[240]{0:T(256)}, f32[240]{0:T(256)S(1)}, u32[]{:S(2)}) copy-start(f32[240]{0:T(256)S(1)} %get-tuple-element.199) | copy-start | bytes 2884
  282.9 11.0 %copy-start.82 = (pred[240]{0:T(512)(128)(4,1)}, pred[240]{0:T(512)(128)(4,1)S(1)}, u32[]{:S(2)}) copy-start(pred[240]{0:T(512)(128)(4,1)S(1)} %and.55) | copy-start | bytes 724
  286.0 17.1 %slice-start.4 = ((s8[11010048]{0:T(1024)(128)(4,1)}), s8[2621440]{0:T(1024)(128)(4,1)S(1)}, s32[]{:S(2)}) async-start(s8[11010048]{0:T(1024)(128)(4,1)} %bitcast.95), calls=%async_computation.4 | async-start | bytes 5242880
  286.0 17.1 %slice-start.5 = ((s8[11010048]{0:T(1024)(128)(4,1)}), s8[4194304]{0:T(1024)(128)(4,1)S(1)}, s32[]{:S(2)}) async-start(s8[11010048]{0:T(1024)(128)(4,1)} %bitcast.95), calls=%async_computation.5 | async-start | bytes 8388608
  369.6 12.0 %slice-start.2 = ((s8[4423680]{0:T(1024)(128)(4,1)}), s8[4194304]{0:T(1024)(128)(4,1)S(1)}, s32[]{:S(2)}) async-start(s8[4423680]{0:T(1024)(128)(4,1)} %bitcast.88), calls=%async_computation.2 | async-start | bytes 8388608
  371.1 10.5 %slice-start.3 = ((s8[4423680]{0:T(1024)(128)(4,1)}), s8[229376]{0:T(1024)(128)(4,1)S(1)}, s32[]{:S(2)}) async-start(s8[4423680]{0:T(1024)(128)(4,1)} %bitcast.88), calls=%async_computation.3 | async-start | bytes 458752
  371.1 10.5 %copy-start.24 = (f32[240,768]{1,0:T(8,128)S(1)}, f32[240,768]{1,0:T(8,128)}, u32[]{:S(2)}) copy-start(f32[240,768]{1,0:T(8,128)} %copy-done.22) | copy-start | bytes 2211844
  421.5 133.0 %copy-start.80 = (f32[24,14]{0,1:T(8,128)S(1)}, f32[24,14]{0,1:T(8,128)}, u32[]{:S(2)}) copy-start(f32[24,14]{0,1:T(8,128)} %param.46) | copy-start | bytes 4036
  421.5 133.1 %copy-start.81 = (f32[24,14]{0,1:T(8,128)S(1)}, f32[24,14]{0,1:T(8,128)}, u32[]{:S(2)}) copy-start(f32[24,14]{0,1:T(8,128)} %param.47) | copy-start | bytes 4036
  421.5 133.2 %copy-start.59 = (f32[24,14]{0,1:T(8,128)S(1)}, f32[24,14]{0,1:T(8,128)}, u32[]{:S(2)}) copy-start(f32[24,14]{0,1:T(8,128)} %param.45) | copy-start | bytes 4036
  421.5 136.9 %copy-start.47 = (f32[24,768]{1,0:T(8,128)S(1)}, f32[24,768]{1,0:T(8,128)}, u32[]{:S(2)}) copy-start(f32[24,768]{1,0:T(8,128)} %param.42) | copy-start | bytes 221188
  421.5 136.9 %copy-start.54 = (f32[24,768]{1,0:T(8,128)S(1)}, f32[24,768]{1,0:T(8,128)}, u32[]{:S(2)}) copy-start(f32[24,768]{1,0:T(8,128)} %param.44) | copy-start | bytes 221188
  421.6 136.9 %copy-start.55 = (f32[24,768]{1,0:T(8,128)S(1)}, f32[24,768]{1,0:T(8,128)}, u32[]{:S(2)}) copy-start(f32[24,768]{1,0:T(8,128)} %param.43) | copy-start | bytes 221188
  421.6 137.6 %copy-start.32 = (f32[96,768]{1,0:T(8,128)S(1)}, f32[96,768]{1,0:T(8,128)}, u32[]{:S(2)}) copy-start(f32[96,768]{1,0:T(8,128)} %param.39) | copy-start | bytes 884740
  421.6 137.6 %copy-start.43 = (f32[96,768]{1,0:T(8,128)S(1)}, f32[96,768]{1,0:T(8,128)}, u32[]{:S(2)}) copy-start(f32[96,768]{1,0:T(8,128)} %param.41) | copy-start | bytes 884740
  421.6 137.6 %copy-start.44 = (f32[96,768]{1,0:T(8,128)S(1)}, f32[96,768]{1,0:T(8,128)}, u32[]{:S(2)}) copy-start(f32[96,768]{1,0:T(8,128)} %param.40) | copy-start | bytes 884740
  (102 other events, 539.5 us)
